TPU v7x, 128 devices: a whole 4x4x4 slice. The times are simulated.
128 devices in a mesh: row: 8 (over y, core), col: 16 (over x, z).
Axes of the slice: x: 4, y: 4, z: 4, core: 2. Of those that a mesh axis runs over, the one named last changes fastest.
Arguments:
- panel: float32 [8192, 512], P('row'), may hold values from -32 to 32, as said below
- trailing: float32 [8192, 8192], P('row', 'col'), may hold values from -86 to 86
Outputs:
- trailing_new: float32 [8192, 8192], P('row', 'col')
- reflectors: float32 [8192, 512], P('row')
Inputs may be any that keep to these rules, and one draw needn't show every extreme that they name: The diagonal entries of the panel's top 512 rows are positive and dominate the other entries of their columns in that block.
All inputs are finite; a program needn't handle non-finite values.
Results may differ from a plain program's by a relative error of at most 0.00014.
Values sent between devices are 32-bit elements; how exact they have to be, the bound alone decides.
A program may use at most 128 MiB of HBM per device.

v0:
```python
import jax
import jax.numpy as jnp
from jax import lax
from jax.sharding import PartitionSpec as P


def from_root(block, axis, source):
    block = jnp.where(lax.axis_index(axis) == source, block, jnp.zeros_like(block))
    return lax.psum(block, axis)


def mult(left, right):
    return jnp.dot(left, right, precision=lax.Precision.HIGHEST)


def inner_rows(left, right):
    return lax.dot_general(left, right, (((0,), (0,)), ((), ())), precision=lax.Precision.HIGHEST)


def outer_cols(left, right):
    return lax.dot_general(left, right, (((1,), (1,)), ((), ())), precision=lax.Precision.HIGHEST)


def leaf_lu(matrix):
    order = matrix.shape[0]
    positions = jnp.arange(order, dtype=jnp.int32)

    def eliminate(step, current):
        step = step.astype(jnp.int32)
        column = lax.dynamic_index_in_dim(current, step, 1, keepdims=False)
        row_vec = lax.dynamic_index_in_dim(current, step, 0, keepdims=False)
        pivot = lax.dynamic_index_in_dim(row_vec, step, 0, keepdims=False)
        below = positions > step
        factors = jnp.where(below, column / pivot, jnp.zeros_like(column))
        right = jnp.where(below, row_vec, jnp.zeros_like(row_vec))
        current = current - factors[:, None] * right[None, :]
        current = jnp.where(
            below[:, None] & (positions == step)[None, :], factors[:, None], current
        )
        return current

    current = lax.fori_loop(0, order, eliminate, matrix)
    lower_unit = jnp.tril(current, -1) + jnp.eye(order, dtype=matrix.dtype)
    return (lower_unit, jnp.triu(current))


def lu_unpivoted(matrix):
    order = matrix.shape[0]
    leaf = min(128, order)
    lower_unit = jnp.zeros_like(matrix)
    upper_factor = jnp.zeros_like(matrix)
    rest = matrix
    for start in range(0, order, leaf):
        lower_one, upper_one = leaf_lu(rest[:leaf, :leaf])
        lower_unit = lower_unit.at[start : start + leaf, start : start + leaf].set(lower_one)
        upper_factor = upper_factor.at[start : start + leaf, start : start + leaf].set(upper_one)
        if start + leaf < order:
            upper_side = jax.scipy.linalg.solve_triangular(
                lower_one, rest[:leaf, leaf:], lower=True, unit_diagonal=True
            )
            lower_side = jax.scipy.linalg.solve_triangular(
                upper_one.T, rest[leaf:, :leaf].T, lower=True
            ).T
            upper_factor = upper_factor.at[start : start + leaf, start + leaf :].set(upper_side)
            lower_unit = lower_unit.at[start + leaf :, start : start + leaf].set(lower_side)
            rest = rest[leaf:, leaf:] - mult(lower_side, upper_side)
    return (lower_unit, upper_factor)


def factor_panel(gram_sum, top_block):
    width = gram_sum.shape[0]
    chol_lower = jnp.linalg.cholesky(gram_sum)
    q_top = jax.scipy.linalg.solve_triangular(chol_lower, top_block.T, lower=True).T
    lower_unit, upper_factor = lu_unpivoted(q_top + jnp.eye(width, dtype=gram_sum.dtype))
    t_factor = jax.scipy.linalg.solve_triangular(
        lower_unit, upper_factor.T, lower=True, unit_diagonal=True
    ).T
    return (chol_lower, upper_factor, t_factor)


def row_picks(count, first_row, width):
    row_ids = first_row + lax.broadcasted_iota(jnp.int32, (count, width), 0)
    col_ids = lax.broadcasted_iota(jnp.int32, (count, width), 1)
    return (row_ids == col_ids).astype(jnp.float32)


def local_terms(rows, first_row, width):
    picks = row_picks(rows.shape[0], first_row, width)
    return (inner_rows(rows, rows), inner_rows(picks, rows))


def reflect_rows(rows, first_row, chol_lower, upper_factor):
    width = rows.shape[1]
    q_rows = jax.scipy.linalg.solve_triangular(chol_lower, rows.T, lower=True).T
    picks = row_picks(rows.shape[0], first_row, width)
    return jax.scipy.linalg.solve_triangular(upper_factor.T, (q_rows + picks).T, lower=True).T


def on_device(panel, trailing):
    rows_dev = panel.shape[0]
    width = panel.shape[1]
    col_rows = trailing.shape[1]
    fanout = lax.axis_size("col") // lax.axis_size("row")
    row_index = lax.axis_index("row")
    col_index = lax.axis_index("col")
    share = rows_dev // lax.axis_size("col")
    piece = lax.dynamic_slice_in_dim(panel, col_index * share, share, 0)
    first_row = row_index * rows_dev + col_index * share
    gram_sum, top_block = lax.psum(local_terms(piece, first_row, width), ("row", "col"))
    chol_lower, upper_factor, t_factor = factor_panel(gram_sum, top_block)
    vec_share = reflect_rows(piece, first_row, chol_lower, upper_factor)
    reflectors = lax.all_gather(vec_share, "col", axis=0, tiled=True)
    owner_row = col_index // fanout
    vec_slice = lax.dynamic_slice_in_dim(reflectors, col_index % fanout * col_rows, col_rows, 0)
    vec_cols = from_root(vec_slice, "row", owner_row)
    scaled_cols = mult(vec_cols, t_factor)
    scaled_rows = mult(reflectors, t_factor)
    image_rows = lax.psum(mult(trailing, scaled_cols), "col")
    curv = lax.psum(inner_rows(scaled_rows, image_rows), "row")
    update_rows = image_rows - 0.5 * mult(reflectors, curv)
    upd_slice = lax.dynamic_slice_in_dim(update_rows, col_index % fanout * col_rows, col_rows, 0)
    update_cols = from_root(upd_slice, "row", owner_row)
    trailing_new = (
        trailing - outer_cols(reflectors, update_cols) - outer_cols(update_rows, vec_cols)
    )
    return (trailing_new, reflectors)


def solution(mesh):
    return jax.shard_map(
        on_device,
        mesh=mesh,
        in_specs=(P("row", None), P("row", "col")),
        out_specs=(P("row", "col"), P("row", None)),
        check_vma=False,
    )
```

profile of v0, /device:TPU:0, one launch (start us, length us, event | category | flops | bytes accessed | tf_op | source)
XLA Modules:
  0.0 1642.5 jit_solution(8168891253101165737)
XLA Ops:
  15.6 151.3 %all-reduce.18.cloned.1.call-done = (f32[512,512]{1,0:T(8,128)}, f32[512,512]{0,1:T(8,128)}) async-done(((f32[512,512]{1,0:T(8,128)}, f32[512,512]{0,1:T(8,128)}), (f32[512,512]{1,0:T(8,128)}, f32[512,512]{0,1:T(8,128)})) %all-reduce.18.cloned.1.call-update) | async-done | bytes 2097168 | tf_op jit(solution)/shard_map/psum | solution.py:109
  166.8 2.6 copy.9
  171.9 11.7 cholesky.108
  183.9 9.8 custom-call.62
  196.3 11.7 cholesky.224
  208.2 10.1 custom-call.63
  219.9 11.7 cholesky.245
  231.9 9.8 custom-call.64
  243.2 11.9 cholesky.262
  260.6 11.2 while.92
  271.8 39.3 %custom-call.65 = f32[4,128,128]{1,2,0:T(8,128)S(1)} custom-call(f32[4,128,128]{2,1,0:T(8,128)S(1)} %get-tuple-element.602), custom_call_target="InvertDiagBlocksLowerTriangular" | custom-call | tf_op jit(solution)/shard_map/jit(_solve_triangular)/triangular_solve | solution.py:73
  319.5 210.1 %while.94 = (s32[]{:T(128)}, f32[128,128]{0,1:T(8,128)S(1)}, s32[]{:T(128)}, s32[]{:T(128)}, s32[]{:T(128)}) while((s32[]{:T(128)}, f32[128,128]{0,1:T(8,128)S(1)}, s32[]{:T(128)}, s32[]{:T(128)}, s32[]{:T(128)}) %tuple.305), condition=%wide.region_11.12_spmd.clone.clone, body=%wide.region_10.11_spmd.clone.clone.sunk | while | flops 66435 | bytes 267881 | solution.py:42
  531.3 9.8 custom-call.67
  542.5 11.3 custom-call.66
  553.8 3.8 fusion.42
  559.1 193.7 %while.95 = (s32[]{:T(128)}, f32[128,128]{0,1:T(8,128)S(1)}, s32[]{:T(128)}, s32[]{:T(128)}, s32[]{:T(128)}) while((s32[]{:T(128)}, f32[128,128]{0,1:T(8,128)S(1)}, s32[]{:T(128)}, s32[]{:T(128)}, s32[]{:T(128)}) %tuple.308), condition=%wide.region_14.15_spmd.clone.clone, body=%wide.region_13.14_spmd.clone.clone.sunk | while | flops 66435 | bytes 267881 | solution.py:42
  754.1 10.4 custom-call.69
  768.6 4.4 scatter.49
  773.7 9.8 custom-call.68
  786.1 177.0 %while.96 = (s32[]{:T(128)}, f32[128,128]{0,1:T(8,128)S(1)}, s32[]{:T(128)}, s32[]{:T(128)}, s32[]{:T(128)}) while((s32[]{:T(128)}, f32[128,128]{0,1:T(8,128)S(1)}, s32[]{:T(128)}, s32[]{:T(128)}, s32[]{:T(128)}) %tuple.311), condition=%wide.region_16.17_spmd.clone.clone, body=%wide.region_15.16_spmd.clone.clone.sunk | while | flops 66435 | bytes 267881 | solution.py:42
  966.9 10.6 custom-call.71
  978.6 10.6 custom-call.70
  989.9 199.7 %while.97 = (s32[]{:T(128)}, f32[128,128]{0,1:T(8,128)S(1)}, s32[]{:T(128)}, s32[]{:T(128)}, s32[]{:T(128)}) while((s32[]{:T(128)}, f32[128,128]{0,1:T(8,128)S(1)}, s32[]{:T(128)}, s32[]{:T(128)}, s32[]{:T(128)}) %tuple.314), condition=%wide.region_18.19_spmd.clone.clone, body=%wide.region_17.18_spmd.clone.clone.sunk | while | flops 66435 | bytes 267881 | solution.py:42
  1193.7 14.8 while.98
  1194.4 2.3 dynamic-slice.168
  1198.1 2.3 dynamic-slice.168
  1201.8 2.3 dynamic-slice.168
  1208.5 41.1 %custom-call.75 = f32[4,128,128]{1,2,0:T(8,128)} custom-call(f32[4,128,128]{2,1,0:T(8,128)} %get-tuple-element.682), custom_call_target="InvertDiagBlocksLowerTriangular" | custom-call | tf_op jit(solution)/shard_map/jit(_solve_triangular)/triangular_solve | solution.py:96
  1261.5 2.4 convert_add_fusion
  1263.9 11.7 while.93
  1264.6 2.3 bitcast_dynamic-update-slice_fusion.10
  1267.5 2.3 bitcast_dynamic-update-slice_fusion.10
  1270.5 2.3 bitcast_dynamic-update-slice_fusion.10
  1275.6 39.9 %custom-call.72 = f32[4,128,128]{1,2,0:T(8,128)} custom-call(f32[4,128,128]{2,1,0:T(8,128)S(1)} %get-tuple-element.610), custom_call_target="InvertDiagBlocksLowerTriangular" | custom-call | tf_op jit(solution)/shard_map/jit(_solve_triangular)/triangular_solve | solution.py:75
  1320.2 2.6 convolution_subtract_fusion.1
  1322.9 2.3 dynamic-slice_select_fusion.1
  1326.8 2.6 convolution_subtract_fusion.6
  1331.4 54.7 %all-reduce.10.cloned.1.call-done = f32[512,512]{1,0:T(8,128)} async-done(((f32[512,512]{1,0:T(8,128)}), f32[512,512]{1,0:T(8,128)}) %all-reduce.10.cloned.1.call-update) | async-done | bytes 1048592 | tf_op jit(solution)/shard_map/psum | solution.py:9
  1386.0 3.4 fusion.30
  1389.5 4.9 convolution_bitcast_fusion
  1395.5 6.4 fusion.29
  1401.8 82.3 %all-reduce.12.cloned.1.call-done = f32[1024,512]{1,0:T(8,128)} async-done(((f32[1024,512]{1,0:T(8,128)}), f32[1024,512]{1,0:T(8,128)}) %all-reduce.12.cloned.1.call-update) | async-done | bytes 2097168 | tf_op jit(solution)/shard_map/psum | solution.py:118
  1484.2 6.7 fusion.151
  1491.2 61.7 %all-reduce.14.cloned.1.call-done = f32[512,512]{1,0:T(8,128)} async-done(((f32[512,512]{1,0:T(8,128)}), f32[512,512]{1,0:T(8,128)}) %all-reduce.14.cloned.1.call-update) | async-done | bytes 1048592 | tf_op jit(solution)/shard_map/psum | solution.py:119
  1552.8 6.1 multiply_subtract_fusion
  1561.3 61.9 %all-reduce.16.cloned.1.call-done = f32[512,512]{1,0:T(8,128)} async-done(((f32[512,512]{1,0:T(8,128)}), f32[512,512]{1,0:T(8,128)}) %all-reduce.16.cloned.1.call-update) | async-done | bytes 1048592 | tf_op jit(solution)/shard_map/psum | solution.py:9
  1623.3 5.5 fusion.152
  1628.8 5.0 subtract_subtract_fusion
  (3278 shorter events, 851.1 us)
Async XLA Ops:
  7.2 1.6 copy-start
  7.2 159.6 %all-reduce.18.cloned.1.call-start = ((), (), s32[]{:S(2)}) async-start(), calls=%async_computation.5 | async-start | bytes 4194304 | tf_op jit(solution)/shard_map/psum | solution.py:109
  8.8 5.5 copy-start.22
  12.4 1310.4 %all-gather.2.cloned.1.call-start = ((), (), s32[]{:S(2)}) async-start(), calls=%async_computation | async-start | bytes 2228224 | tf_op jit(solution)/shard_map/all_gather | solution.py:112
  166.8 2.6 copy-start.11
  170.9 1.0 copy-start.15
  218.6 41.9 %copy-start.21 = (s32[4]{0:T(128)S(1)}, s32[4]{0:T(128)}, u32[]{:S(2)}) copy-start(s32[4]{0:T(128)} %iota_multiply_fusion.1) | copy-start | bytes 52
  311.1 6.9 copy-start.18
  318.5 1.0 copy-start.9
  529.7 27.9 %copy-start.10 = (f32[512,512]{0,1:T(8,128)S(1)}, f32[512,512]{0,1:T(8,128)}, u32[]{:S(2)}) copy-start(f32[512,512]{0,1:T(8,128)} %copy-done.9) | copy-start | bytes 3145732
  558.3 0.8 copy-start.16
  767.6 1.0 copy-start.12
  1191.9 57.7 %copy-start.19 = (f32[4,128,128]{1,2,0:T(8,128)S(1)}, f32[4,128,128]{1,2,0:T(8,128)}, u32[]{:S(2)}) copy-start(f32[4,128,128]{1,2,0:T(8,128)} %copy-done.18) | copy-start | bytes 786436
  1249.6 9.5 copy-start.20
  1261.4 124.6 %all-reduce.10.cloned.1.call-start = ((), (), s32[]{:S(2)}) async-start(), calls=%async_computation.1 | async-start | bytes 2097152 | tf_op jit(solution)/shard_map/psum | solution.py:9
  1319.5 0.7 copy-start.6
  1325.2 159.0 %all-reduce.12.cloned.1.call-start = ((), (), s32[]{:S(2)}) async-start(), calls=%async_computation.2 | async-start | bytes 4194304 | tf_op jit(solution)/shard_map/psum | solution.py:118
  1326.8 2.6 copy-start.13
  1386.0 3.4 copy-start.4
  1394.3 0.9 copy-start.7
  1394.3 1.0 copy-start.14
  1394.3 1.1 copy-start.17
  1394.4 158.5 %all-reduce.14.cloned.1.call-start = ((), (), s32[]{:S(2)}) async-start(), calls=%async_computation.3 | async-start | bytes 2097152 | tf_op jit(solution)/shard_map/psum | solution.py:119
  1490.9 132.4 %all-reduce.16.cloned.1.call-start = ((), (), s32[]{:S(2)}) async-start(), calls=%async_computation.4 | async-start | bytes 2097152 | tf_op jit(solution)/shard_map/psum | solution.py:9
  1558.9 1.3 copy-start.2
  1561.3 67.4 %copy-start.8 = (f32[512,512]{1,0:T(8,128)S(1)}, f32[512,512]{1,0:T(8,128)}, u32[]{:S(2)}) copy-start(f32[512,512]{1,0:T(8,128)} %all-reduce.10.cloned.1.call-done) | copy-start | bytes 3145732
  1623.3 5.5 copy-start.3
  1623.3 5.5 copy-start.5
  1628.8 5.1 copy-start.1
Sparse Core Ops, SparseCore 0:
  13.6 153.1 all-reduce.17
  1261.5 43.6 all-gather.1
  1325.3 60.7 all-reduce.9
  1394.5 89.6 all-reduce.11
  1491.0 61.8 all-reduce.13
  1561.5 61.7 all-reduce.15
where the time goes:
time: 1660 us; the launch traced here: 1640 us
  other arithmetic  668 us (40%)
  local copies, waits for them, and re-layouts  426 us (26%)
  waiting for transfers between devices  412 us (25%)
  matrix products  88.1 us (5%)
  loops' own time  29.5 us (2%)
  between operations  17.9 us (1%)
    broadcast_in_dim x512, other arithmetic, eliminate(): jnp.where(below[:, None] & (positions == step)[None, :], factors[:, None]...  326 us
    dynamic_slice x512, local copies, waits for them, and re-layouts, eliminate(): pivot = lax.dynamic_index_in_dim(row_vec, step, 0, keepdims=False)  316 us
    psum x1, waiting for transfers between devices, on_device(): lax.psum(local_terms(piece, first_row, width), ('row', 'col'))  151 us
    psum x2, waiting for transfers between devices, from_root(): return lax.psum(block, axis)  117 us
    psum x1, waiting for transfers between devices, on_device(): image_rows = lax.psum(mult(trailing, scaled_cols), 'col')  82.3 us
    another operation x18, other arithmetic, factor_panel(): chol_lower = jnp.linalg.cholesky(gram_sum)  78.8 us
    psum x1, waiting for transfers between devices, on_device(): curv = lax.psum(inner_rows(scaled_rows, image_rows), 'row')  61.7 us
    select_n x512, other arithmetic, eliminate(): jnp.where(below[:, None] & (positions == step)[None, :], factors[:, None]...  54.2 us
  transfers between devices with their start and end apart: 6, of which 5 were waited for; matrix products, arithmetic and copies ran while one was open for 5% of the time, Pallas kernels for 0%

commit v1 on v0

v1 whole, which is shorter than its diff:
```python
import functools
import jax, jax.numpy as jnp
from jax import lax
from jax.experimental import pallas as pl
from jax.experimental.pallas import tpu as pltpu
from jax.sharding import PartitionSpec as P

HI = lax.Precision.HIGHEST
B = 64
NB = 512
NPH = NB // B


def dot(a, b):
    return lax.dot_general(a, b, (((1,), (0,)), ((), ())), precision=HI, preferred_element_type=jnp.float32)


def dot_t(a, b):
    return lax.dot_general(a, b, (((0,), (0,)), ((), ())), precision=HI, preferred_element_type=jnp.float32)


def eliminate(e_ref, count):
    sub = lax.broadcasted_iota(jnp.int32, (8, 128), 0)
    rows = [[e_ref[t, 8 * i : 8 * i + 8, :] for i in range(B // 8)] for t in range(count)]

    def lane(v, k):
        return jnp.broadcast_to(v[:, k : k + 1], (8, 128))

    def row(v, k):
        return jnp.broadcast_to(v[k : k + 1, :], (8, 128))

    for jb in range(B // 8):
        full = [rows[t][jb] for t in range(count)]
        cols = [[lane(full[t], 8 * jb + m) for m in range(8)] for t in range(count)]
        kept = list(full)
        for m in range(8):
            for t in range(count):
                here = sub == m
                col = cols[t][m]
                rp = 1.0 / row(col, m)
                if m:
                    kept[t] = jnp.where(here, full[t], kept[t])
                scaled = row(full[t], m) * rp
                full[t] = jnp.where(here, scaled, full[t] - col * scaled)
                for k in range(m + 1, 8):
                    scaled = row(cols[t][k], m) * rp
                    cols[t][k] = jnp.where(here, scaled, cols[t][k] - col * scaled)
        for t in range(count):
            rows[t][jb] = kept[t]
            spread = [row(full[t], m) for m in range(8)]
            for i in range(jb + 1, B // 8):
                terms = [lane(rows[t][i], 8 * jb + m) * spread[m] for m in range(8)]
                while len(terms) > 1:
                    terms = [terms[k] + terms[k + 1] for k in range(0, len(terms), 2)]
                rows[t][i] = rows[t][i] - terms[0]
    for t in range(count):
        for i in range(B // 8):
            e_ref[t, 8 * i : 8 * i + 8, :] = rows[t][i]


def factor_kernel(g_ref, a1_ref, r_ref, rit_ref, lui_ref, mi_ref, x_ref, s_ref, e_ref):
    r_i = lax.broadcasted_iota(jnp.int32, (B, B), 0)
    c_i = lax.broadcasted_iota(jnp.int32, (B, B), 1)
    eye = (r_i == c_i).astype(jnp.float32)
    x_ref[...] = g_ref[...]
    s_ref[...] = a1_ref[...]
    r_ref[...] = jnp.zeros_like(r_ref)
    rit_ref[...] = jnp.zeros_like(rit_ref)
    lui_ref[...] = jnp.zeros_like(lui_ref)
    mi_ref[...] = jnp.zeros_like(mi_ref)
    for t in range(3):
        e_ref[t, :, :B] = eye
        e_ref[t, :, B:] = eye

    def diag(v):
        return jnp.sum(jnp.where(r_i == c_i, v, 0.0), axis=1, keepdims=True)

    def pre(p):
        a, b = p * B, (p + 1) * B
        if p < NPH:
            e_ref[0, :, :B] = x_ref[a:b, a:b]
            e_ref[0, :, B:] = eye
        if p > 0:
            a, b = a - B, b - B
            block = s_ref[a:b, a:b]
            e_ref[1, :, :B] = block
            e_ref[1, :, B:] = eye
            e_ref[2, :, :B] = block.T
            e_ref[2, :, B:] = eye

    def post(p):
        a, b = p * B, (p + 1) * B
        if p < NPH:
            left = e_ref[0, :, :B]
            rs = lax.rsqrt(diag(left))
            linv = rs * e_ref[0, :, B:]
            rpp = jnp.where(r_i <= c_i, rs * left, 0.0)
            r_ref[a:b, a:b] = rpp
            rit_ref[a:b, a:b] = linv
            if p:
                rit_ref[a:b, :a] = dot(linv, rit_ref[a:b, :a])
            s_ref[a:b, a:b] += rpp
            if b < NB:
                rrow = dot(linv, x_ref[a:b, b:])
                r_ref[a:b, b:] = rrow
                s_ref[a:b, b:] += rrow
                x_ref[b:, b:] -= dot_t(rrow, rrow)
                rit_ref[b:, :b] -= dot_t(rrow, rit_ref[a:b, :b])
        if p > 0:
            a, b = a - B, b - B
            lui = e_ref[1, :, B:]
            mit = (1.0 / diag(e_ref[2, :, :B])) * e_ref[2, :, B:]
            mi = mit.T
            lui_ref[a:b, a:b] = lui
            mi_ref[a:b, a:b] = mi
            if a:
                lui_ref[a:b, :a] = dot(lui, lui_ref[a:b, :a])
                mi_ref[:a, a:b] = dot(mi_ref[:a, a:b], mi)
            if b < NB:
                mrow = dot(lui, s_ref[a:b, b:])
                lucol = dot(s_ref[b:, a:b], mi)
                s_ref[b:, b:] -= dot(lucol, mrow)
                lui_ref[b:, :b] -= dot(lucol, lui_ref[a:b, :b])
                mi_ref[:b, b:] -= dot(mi_ref[:b, a:b], mrow)

    def phase(ph, carry):
        for p in range(NPH + 1):
            pl.when(ph == p)(functools.partial(pre, p))
        eliminate(e_ref, 3)
        for p in range(NPH + 1):
            pl.when(ph == p)(functools.partial(post, p))
        return carry

    lax.fori_loop(0, NPH + 1, phase, 0)


def factor(g, a1):
    sq = jax.ShapeDtypeStruct((NB, NB), jnp.float32)
    vm = pl.BlockSpec(memory_space=pltpu.VMEM)
    return pl.pallas_call(
        factor_kernel,
        out_shape=[sq] * 4,
        in_specs=[vm] * 2,
        out_specs=[vm] * 4,
        scratch_shapes=[
            pltpu.VMEM((NB, NB), jnp.float32),
            pltpu.VMEM((NB, NB), jnp.float32),
            pltpu.VMEM((3, B, 2 * B), jnp.float32),
        ],
        compiler_params=pltpu.CompilerParams(vmem_limit_bytes=50 * 1024 * 1024),
        name="factor",
    )(g, a1)


def mult(left, right):
    return jnp.dot(left, right, precision=lax.Precision.HIGHEST)


def inner_rows(left, right):
    return lax.dot_general(left, right, (((0,), (0,)), ((), ())), precision=lax.Precision.HIGHEST)


def outer_cols(left, right):
    return lax.dot_general(left, right, (((1,), (1,)), ((), ())), precision=lax.Precision.HIGHEST)


def from_root(block, axis, source):
    block = jnp.where(lax.axis_index(axis) == source, block, jnp.zeros_like(block))
    return lax.psum(block, axis)


def on_device(panel, trailing):
    rows_dev = panel.shape[0]
    col_rows = trailing.shape[1]
    fanout = lax.axis_size("col") // lax.axis_size("row")
    row_index = lax.axis_index("row")
    col_index = lax.axis_index("col")
    owner_row = col_index // fanout
    place = col_index % fanout * col_rows
    gram = inner_rows(panel, panel)
    top = jnp.where(row_index == 0, panel[:NB], jnp.zeros((NB, NB), jnp.float32))
    gram, top = lax.psum((gram, top), "row")
    panel_cols = from_root(lax.dynamic_slice_in_dim(panel, place, col_rows, 0), "row", owner_row)
    r_up, rit, lui, mi = factor(gram, top)
    k2 = mult(rit.T, lui.T)
    shifted = panel.at[:NB].add(jnp.where(row_index == 0, r_up, jnp.zeros_like(r_up)))
    shifted_cols = panel_cols + jnp.where(col_index == 0, r_up, jnp.zeros_like(r_up))
    reflectors = mult(shifted, mi)
    scaled_rows = mult(shifted, k2)
    vec_cols = mult(shifted_cols, mi)
    scaled_cols = mult(shifted_cols, k2)
    image_rows = lax.psum(mult(trailing, scaled_cols), "col")
    curv = lax.psum(inner_rows(scaled_rows, image_rows), "row")
    update_rows = image_rows - 0.5 * mult(reflectors, curv)
    upd_slice = lax.dynamic_slice_in_dim(update_rows, place, col_rows, 0)
    update_cols = from_root(upd_slice, "row", owner_row)
    trailing_new = (
        trailing - outer_cols(reflectors, update_cols) - outer_cols(update_rows, vec_cols)
    )
    return (trailing_new, reflectors)


def solution(mesh):
    return jax.shard_map(
        on_device,
        mesh=mesh,
        in_specs=(P("row", None), P("row", "col")),
        out_specs=(P("row", "col"), P("row", None)),
        check_vma=False,
    )
```

time: 1660 us -> 390 us (0.23)
  other arithmetic: 668 us -> 3.18 us
  local copies, waits for them, and re-layouts: 426 us -> 2.95 us
  waiting for transfers between devices: 412 us -> 269 us
  Pallas kernels: 0 us -> 42.6 us
  matrix products: 88.1 us -> 52.8 us
  loops' own time: 29.5 us -> 0 us
    broadcast_in_dim x512 -> x0, other arithmetic: 326 us -> none  [eliminate(): jnp.where(below[:, None] & (positions == step)[None, :], factors[:, None]...]
    dynamic_slice x512 -> x0, local copies, waits for them, and re-layouts: 316 us -> none  [eliminate(): pivot = lax.dynamic_index_in_dim(row_vec, step, 0, keepdims=False)]
    another operation x37 -> x0, other arithmetic: 270 us -> none  [the longest x18 78.8 us: factor_panel(): chol_lower = jnp.linalg.cholesky(gram_sum)]
    psum x1, waiting for transfers between devices: 151 us -> 71.7 us  [on_device(): gram, top = lax.psum((gram, top), 'row')]
    psum x2 -> x1, waiting for transfers between devices: 117 us -> 57.4 us  [from_root(): return lax.psum(block, axis)]
    select_n x512 -> x0, other arithmetic: 54.2 us -> none  [eliminate(): jnp.where(below[:, None] & (positions == step)[None, :], factors[:, None]...]
    while x516 -> x0, local copies, waits for them, and re-layouts: 45.4 us -> none
    another operation x40 -> x0, matrix products: 44.2 us -> none  [the longest x7 12.6 us: factor_panel(): jax.scipy.linalg.solve_triangular(lower_unit, upper_factor.T, lower=True,...]
  transfers between devices with their start and end apart: 6 -> 4, of which waited for: 5 -> 4; matrix products, arithmetic and copies ran while one was open for 5% -> 4% of each run, Pallas kernels for 0% -> 0%
where the time goes in v1:
time: 390 us; the launch traced here: 386 us
  waiting for transfers between devices  269 us (69%)
  matrix products  52.8 us (14%)
  Pallas kernels  42.6 us (11%)
  between operations  14.3 us (4%)
    psum x1, waiting for transfers between devices, on_device(): image_rows = lax.psum(mult(trailing, scaled_cols), 'col')  84.4 us
    psum x1, waiting for transfers between devices, on_device(): gram, top = lax.psum((gram, top), 'row')  71.7 us
    psum x1, waiting for transfers between devices, from_root(): return lax.psum(block, axis)  57.4 us
    psum x1, waiting for transfers between devices, on_device(): curv = lax.psum(inner_rows(scaled_rows, image_rows), 'row')  55.7 us
    pallas_call x1, Pallas kernels, factor(): pl.pallas_call(factor_kernel, out_shape=[sq] * 4, in_specs=[vm] * 2, out_...  42.6 us
    dot_general x7, matrix products, mult(): return jnp.dot(left, right, precision=lax.Precision.HIGHEST)  31.5 us
    dot_general x2, matrix products, inner_rows(): lax.dot_general(left, right, (((0,), (0,)), ((), ())), precision=lax.Prec...  11.2 us
    dot_general x2, matrix products, outer_cols(): lax.dot_general(left, right, (((1,), (1,)), ((), ())), precision=lax.Prec...  10.1 us
  transfers between devices with their start and end apart: 4, of which 4 were waited for; matrix products, arithmetic and copies ran while one was open for 4% of the time, Pallas kernels for 0%

profile of v1, /device:TPU:0, one launch (start us, length us, event | category | flops | bytes accessed | tf_op | source)
XLA Modules:
  0.0 385.6 jit_solution(11810398861580732307)
XLA Ops:
  7.2 0.0 all-reduce.12.cloned.1.call-start
  7.2 1.6 copy.14
  8.8 4.5 %fusion.4 = f32[512,512]{1,0:T(8,128)} fusion(f32[1024,512]{1,0:T(8,128)S(1)} %copy.14), kind=kOutput, calls=%fused_computation.12 | convolution fusion | flops 3221225472 | bytes 3145728 | tf_op jit(solution)/shard_map/dot_general | solution.py:160
  13.3 1.6 dynamic-slice_select_fusion.1
  14.9 0.0 all-reduce.12.cloned.1.call-update
  14.9 0.0 all-reduce.6.cloned.1.call-start
  15.0 71.7 %all-reduce.12.cloned.1.call-done = (f32[512,512]{1,0:T(8,128)}, f32[512,512]{1,0:T(8,128)}, f32[512,512]{1,0:T(8,128)}) async-done(((f32[512,512]{1,0:T(8,128)}, f32[512,512]{1,0:T(8,128)}, f32[512,512]{1,0:T(8,128)}), (f32[512,512]{1,0:T(8,128)}, f32[512,512]{1,0:T(8,128)}, f32[512,512]{1,0:T(8,128)})) %all-reduce.12.cloned.1.call-update) | async-done | bytes 3145744 | tf_op jit(solution)/shard_map/psum | solution.py:182
  86.7 42.6 %factor.1 = (f32[512,512]{1,0:T(8,128)S(1)}, f32[512,512]{1,0:T(8,128)S(1)}, f32[512,512]{1,0:T(8,128)S(1)}, f32[512,512]{1,0:T(8,128)}) custom-call(f32[512,512]{1,0:T(8,128)} %get-tuple-element.22.g_ref, f32[512,512]{1,0:T(8,128)} %get-tuple-element.23.a1_ref), custom_call_target="tpu_custom_call" | custom-call | tf_op jit(solution)/shard_map/factor/pallas_call | solution.py:140
  129.3 0.0 copy-start.7
  129.3 3.5 fusion.6
  132.8 0.0 copy-start.3
  132.8 0.0 copy-done.7
  132.8 0.0 copy-start.5
  132.8 1.9 fusion.1
  134.7 0.0 copy-done.3
  134.7 0.0 copy-done.5
  134.8 4.9 %convolution_bitcast_fusion = f32[1024,512]{1,0:T(8,128)} fusion(f32[512,512]{1,0:T(8,128)S(1)} %fusion.1, f32[1024,512]{1,0:T(8,128)S(1)} %copy-done.5), kind=kOutput, calls=%fused_computation.2 | convolution fusion | flops 3221225472 | bytes 5242880 | tf_op jit(solution)/shard_map/dot_general | solution.py:156
  139.6 0.0 all-reduce.6.cloned.1.call-update
  139.7 0.0 all-reduce.8.cloned.1.call-start
  139.7 0.0 copy-start.4
  139.7 0.3 add_dynamic-update-slice_fusion
  140.0 0.9 copy-done.4
  140.9 4.8 %fusion.7 = f32[1024,512]{1,0:T(8,128)} fusion(f32[1024,512]{1,0:T(8,128)S(1)} %add_dynamic-update-slice_fusion, f32[512,512]{1,0:T(8,128)S(1)} %copy-done.4), kind=kOutput, calls=%fused_computation.15 | convolution fusion | flops 3221225472 | bytes 5242880 | tf_op jit(solution)/shard_map/dot_general | solution.py:156
  145.7 84.4 %all-reduce.6.cloned.1.call-done = f32[1024,512]{1,0:T(8,128)} async-done(((f32[1024,512]{1,0:T(8,128)}), f32[1024,512]{1,0:T(8,128)}) %all-reduce.6.cloned.1.call-update) | async-done | bytes 2097168 | tf_op jit(solution)/shard_map/psum | solution.py:192
  230.1 6.7 %fusion.8 = f32[512,512]{1,0:T(8,128)} fusion(f32[1024,512]{1,0:T(8,128)} %fusion.7, f32[1024,512]{1,0:T(8,128)} %all-reduce.6.cloned.1.call-done), kind=kOutput, calls=%fused_computation.16 | convolution fusion | flops 3221225472 | bytes 5242880 | tf_op jit(solution)/shard_map/dot_general | solution.py:160
  236.7 0.0 all-reduce.8.cloned.1.call-update
  236.8 0.3 all-reduce.10.cloned.1.call-start
  237.0 6.0 %fusion.5 = f32[1024,512]{1,0:T(8,128)} fusion(f32[1024,512]{1,0:T(8,128)S(1)} %add_dynamic-update-slice_fusion, f32[512,512]{1,0:T(8,128)} %get-tuple-element.19), kind=kOutput, calls=%fused_computation.13 | convolution fusion | flops 3221225472 | bytes 5242880 | tf_op jit(solution)/shard_map/dot_general | solution.py:156
  243.0 55.7 %all-reduce.8.cloned.1.call-done = f32[512,512]{1,0:T(8,128)} async-done(((f32[512,512]{1,0:T(8,128)}), f32[512,512]{1,0:T(8,128)}) %all-reduce.8.cloned.1.call-update) | async-done | bytes 1048592 | tf_op jit(solution)/shard_map/psum | solution.py:193
  298.7 6.0 %multiply_subtract_fusion = f32[1024,512]{1,0:T(8,128)S(1)} fusion(f32[1024,512]{1,0:T(8,128)} %all-reduce.6.cloned.1.call-done, f32[1024,512]{1,0:T(8,128)} %fusion.5, f32[512,512]{1,0:T(8,128)} %all-reduce.8.cloned.1.call-done), kind=kOutput, calls=%fused_computation.1 | convolution fusion | flops 3222274048 | bytes 7340032 | tf_op jit(solution)/shard_map/dot_general | solution.py:156
  304.8 0.0 copy-start.1
  304.8 1.3 dynamic-slice_select_fusion
  306.0 0.4 copy-done.1
  306.4 0.0 all-reduce.10.cloned.1.call-update
  306.4 0.0 copy-start
  306.5 4.5 %fusion = f32[512,512]{1,0:T(8,128)} fusion(f32[512,512]{1,0:T(8,128)} %get-tuple-element.19, f32[512,512]{1,0:T(8,128)} %get-tuple-element.24, f32[512,512]{1,0:T(8,128)S(1)} %get-tuple-element.18, pred[]{:T(512)S(6)} %eq.15), kind=kOutput, calls=%fused_computation.8 | convolution fusion | flops 1611137024 | bytes 4194305 | tf_op jit(solution)/shard_map/dot_general | solution.py:156
  311.0 0.0 copy-start.8
  311.0 57.4 %all-reduce.10.cloned.1.call-done = f32[512,512]{1,0:T(8,128)} async-done(((f32[512,512]{1,0:T(8,128)}), f32[512,512]{1,0:T(8,128)}) %all-reduce.10.cloned.1.call-update) | async-done | bytes 1048592 | tf_op jit(solution)/shard_map/psum | solution.py:169
  368.4 0.0 copy-done
  368.4 0.0 copy-start.2
  368.4 0.0 copy-start.6
  368.4 4.8 %fusion.9 = f32[1024,512]{1,0:T(8,128)S(1)} fusion(f32[1024,512]{1,0:T(8,128)S(1)} %copy-done, f32[512,512]{1,0:T(8,128)} %all-reduce.10.cloned.1.call-done), kind=kOutput, calls=%fused_computation.17 | convolution fusion | flops 3221225472 | bytes 5242880 | tf_op jit(solution)/shard_map/dot_general | solution.py:164
  373.2 0.0 copy-done.8
  373.3 0.0 copy-done.2
  373.3 0.0 copy-done.6
  373.3 5.3 %subtract_subtract_fusion = f32[1024,512]{1,0:T(8,128)} fusion(f32[1024,512]{1,0:T(8,128)S(1)} %copy-done.6, f32[1024,512]{1,0:T(8,128)S(1)} %fusion.9, f32[1024,512]{1,0:T(8,128)S(1)} %copy-done.2, f32[512,512]{1,0:T(8,128)S(1)} %copy-done.8), kind=kOutput, calls=%fused_computation | convolution fusion | flops 3222274048 | bytes 9437184 | tf_op jit(solution)/shard_map/dot_general | solution.py:164
Async XLA Ops:
  7.2 79.5 %all-reduce.12.cloned.1.call-start = ((), (), s32[]{:S(2)}) async-start(), calls=%async_computation.3 | async-start | bytes 6291456 | tf_op jit(solution)/shard_map/psum | solution.py:182
  14.9 215.2 %all-reduce.6.cloned.1.call-start = ((), (), s32[]{:S(2)}) async-start(), calls=%async_computation | async-start | bytes 4194304 | tf_op jit(solution)/shard_map/psum | solution.py:192
  129.3 3.5 copy-start.7
  132.8 1.9 copy-start.3
  132.8 2.0 copy-start.5
  139.7 159.1 %all-reduce.8.cloned.1.call-start = ((), (), s32[]{:S(2)}) async-start(), calls=%async_computation.1 | async-start | bytes 2097152 | tf_op jit(solution)/shard_map/psum | solution.py:193
  139.7 1.2 copy-start.4
  236.8 131.6 %all-reduce.10.cloned.1.call-start = ((), (), s32[]{:S(2)}) async-start(), calls=%async_computation.2 | async-start | bytes 2097152 | tf_op jit(solution)/shard_map/psum | solution.py:169
  304.8 1.7 copy-start.1
  306.4 61.9 %copy-start = (f32[1024,512]{1,0:T(8,128)S(1)}, f32[1024,512]{1,0:T(8,128)}, u32[]{:S(2)}) copy-start(f32[1024,512]{1,0:T(8,128)} %fusion.5) | copy-start | bytes 6291460
  311.0 62.3 %copy-start.8 = (f32[512,512]{1,0:T(8,128)S(1)}, f32[512,512]{1,0:T(8,128)}, u32[]{:S(2)}) copy-start(f32[512,512]{1,0:T(8,128)} %fusion) | copy-start | bytes 3145732
  368.4 4.9 %copy-start.2 = (f32[1024,512]{1,0:T(8,128)S(1)}, f32[1024,512]{1,0:T(8,128)}, u32[]{:S(2)}) copy-start(f32[1024,512]{1,0:T(8,128)} %copy-done.1) | copy-start | bytes 6291460
  368.4 4.9 %copy-start.6 = (f32[1024,512]{1,0:T(8,128)S(1)}, f32[1024,512]{1,0:T(8,128)}, u32[]{:S(2)}) copy-start(f32[1024,512]{1,0:T(8,128)} %param.5) | copy-start | bytes 6291460
Sparse Core Ops, SparseCore 0:
  15.0 71.6 all-reduce.11
  139.8 90.2 all-reduce.5
  236.9 61.8 all-reduce.7
  306.6 61.7 all-reduce.9

commit v2 on v1

--- a/solution.py
+++ b/solution.py
@@ -6,9 +6,13 @@
 from jax.sharding import PartitionSpec as P
 
 HI = lax.Precision.HIGHEST
+MESH = pl.DeviceIdType.MESH
 B = 64
 NB = 512
 NPH = NB // B
+T = 128
+PAIRS = [(i, j) for i in range(NB // T) for j in range(i, NB // T)]
+PIECE = len(PAIRS) * T // 8
 
 
 def dot(a, b):
@@ -58,12 +62,123 @@
             e_ref[t, 8 * i : 8 * i + 8, :] = rows[t][i]
 
 
-def factor_kernel(g_ref, a1_ref, r_ref, rit_ref, lui_ref, mi_ref, x_ref, s_ref, e_ref):
+def remote(src, dst, sends, recvs, n, device):
+    return pltpu.make_async_remote_copy(
+        src_ref=src, dst_ref=dst, send_sem=sends.at[n], recv_sem=recvs.at[n],
+        device_id=device, device_id_type=MESH,
+    )
+
+
+def gather_kernel_part(panel_ref, x_ref, s_ref, gp, other, half, parts, total, top, sends, recvs):
+    r, c = lax.axis_index("row"), lax.axis_index("col")
+    y, k = lax.div(r, 2), lax.rem(r, 2)
+    x, z = lax.div(c, 4), lax.rem(c, 4)
+    ys = [lax.rem(y + d, 4) for d in range(1, 4)]
+    mate = (2 * y + 1 - k, c)
+    y_mates = [(2 * v + k, c) for v in ys]
+    y_cross = [(2 * v + 1 - k, c) for v in ys]
+    x_mates = [(r, lax.rem(x + d, 4) * 4 + z) for d in range(1, 4)]
+    z_mates = [(r, x * 4 + lax.rem(z + d, 4)) for d in range(1, 4)]
+    peers = [mate] + y_mates + y_cross + x_mates + z_mates
+    barrier = pltpu.get_barrier_semaphore()
+    for peer in peers:
+        pl.semaphore_signal(barrier, inc=1, device_id=peer, device_id_type=MESH)
+
+    for i in range(NB // T):
+        strip = dot_t(panel_ref[:, i * T : (i + 1) * T], panel_ref[:, i * T :])
+        for j in range(i, NB // T):
+            n = PAIRS.index((i, j)) * T
+            done = 0
+            while done < T:
+                q, o = divmod(n + done, PIECE)
+                m = min(T - done, PIECE - o)
+                gp[q, o : o + m, :] = strip[done : done + m, (j - i) * T : (j - i + 1) * T]
+                done += m
+    pl.semaphore_wait(barrier, len(peers))
+
+    first = remote(gp.at[pl.ds(4 * (1 - k), 4)], other, sends, recvs, 0, mate)
+    first.start()
+
+    @pl.when(r == 0)
+    def _():
+        out = []
+        for n, peer in enumerate([(1, c)] + [(2 * v + q, c) for v in range(1, 4) for q in range(2)]):
+            q = 1 if n == 0 else (n - 1) % 2
+            src = panel_ref.at[pl.ds(pl.multiple_of(32 * c + 16 * q, 16), 16)]
+            place = x + 4 * z if q == 0 else z + 4 * x
+            cp = pltpu.make_async_remote_copy(
+                src_ref=src, dst_ref=top.at[q, place], send_sem=sends.at[16 + n], recv_sem=recvs.at[1],
+                device_id=peer, device_id_type=MESH)
+            cp.start()
+            out.append(cp)
+        top[0, x + 4 * z] = panel_ref[pl.ds(pl.multiple_of(32 * c, 16), 16), :]
+        for cp in out:
+            cp.wait_send()
+
+    first.wait()
+    half[...] = gp[pl.ds(4 * k, 4)] + other[...]
+    second = []
+    for d in range(3):
+        cp = remote(half.at[ys[d]], parts.at[d], sends, recvs, 2 + d, y_mates[d])
+        cp.start()
+        second.append(cp)
+
+    mine = jnp.where(k == 0, x + 4 * z, z + 4 * x)
+
+    @pl.when(r > 0)
+    def _():
+        remote(top.at[k, mine], top.at[k, mine], sends, recvs, 1, mate).wait_recv()
+
+    def spread_top(base, src, peers_0, peers_1):
+        cps = []
+        for d in range(3):
+            peer = (r, jnp.where(k == 0, peers_0[d][1], peers_1[d][1]))
+            cp = remote(src, src, sends, recvs, base + d, peer)
+            cp.start()
+            cps.append(cp)
+        return cps
+
+    third = spread_top(5, top.at[k, mine], x_mates, z_mates)
+    for cp in second:
+        cp.wait()
+    total[4 * k + y] = (half[y] + parts[0]) + (parts[1] + parts[2])
+    fourth = []
+    for d in range(3):
+        cp = remote(total.at[4 * k + y], total.at[4 * k + y], sends, recvs, 8 + d, y_mates[d])
+        cp.start()
+        fourth.append(cp)
+    for cp in third:
+        cp.wait()
+    group = pl.ds(4 * jnp.where(k == 0, z, x), 4)
+    fifth = spread_top(11, top.at[k, group], z_mates, x_mates)
+    for cp in fourth:
+        cp.wait()
+    sixth = remote(total.at[pl.ds(4 * k, 4)], total.at[pl.ds(4 * k, 4)], sends, recvs, 14, mate)
+    sixth.start()
+    for cp in fifth:
+        cp.wait()
+    seventh = remote(top.at[k], top.at[k], sends, recvs, 15, mate)
+    seventh.start()
+    sixth.wait()
+    for n, (i, j) in enumerate(PAIRS):
+        done = 0
+        while done < T:
+            q, o = divmod(n * T + done, PIECE)
+            m = min(T - done, PIECE - o)
+            x_ref[i * T + done : i * T + done + m, j * T : (j + 1) * T] = total[q, o : o + m, :]
+            done += m
+    seventh.wait()
+    for a in range(4):
+        for b in range(4):
+            s_ref[32 * (4 * a + b) : 32 * (4 * a + b) + 16, :] = top[0, a + 4 * b]
+            s_ref[32 * (4 * a + b) + 16 : 32 * (4 * a + b) + 32, :] = top[1, b + 4 * a]
+
+
+def factor_kernel(panel_ref, r_ref, rit_ref, lui_ref, mi_ref, x_ref, s_ref, e_ref, gp, other, half, parts, total, top, sends, recvs):
+    gather_kernel_part(panel_ref, x_ref, s_ref, gp, other, half, parts, total, top, sends, recvs)
     r_i = lax.broadcasted_iota(jnp.int32, (B, B), 0)
     c_i = lax.broadcasted_iota(jnp.int32, (B, B), 1)
     eye = (r_i == c_i).astype(jnp.float32)
-    x_ref[...] = g_ref[...]
-    s_ref[...] = a1_ref[...]
     r_ref[...] = jnp.zeros_like(r_ref)
     rit_ref[...] = jnp.zeros_like(rit_ref)
     lui_ref[...] = jnp.zeros_like(lui_ref)
@@ -78,7 +193,8 @@
     def pre(p):
         a, b = p * B, (p + 1) * B
         if p < NPH:
-            e_ref[0, :, :B] = x_ref[a:b, a:b]
+            block = x_ref[a:b, a:b]
+            e_ref[0, :, :B] = jnp.where(r_i <= c_i, block, block.T)
             e_ref[0, :, B:] = eye
         if p > 0:
             a, b = a - B, b - B
@@ -134,22 +250,32 @@
     lax.fori_loop(0, NPH + 1, phase, 0)
 
 
-def factor(g, a1):
+def factor(panel):
     sq = jax.ShapeDtypeStruct((NB, NB), jnp.float32)
     vm = pl.BlockSpec(memory_space=pltpu.VMEM)
+    f32 = jnp.float32
     return pl.pallas_call(
         factor_kernel,
         out_shape=[sq] * 4,
-        in_specs=[vm] * 2,
+        in_specs=[vm],
         out_specs=[vm] * 4,
         scratch_shapes=[
-            pltpu.VMEM((NB, NB), jnp.float32),
-            pltpu.VMEM((NB, NB), jnp.float32),
-            pltpu.VMEM((3, B, 2 * B), jnp.float32),
+            pltpu.VMEM((NB, NB), f32),
+            pltpu.VMEM((NB, NB), f32),
+            pltpu.VMEM((3, B, 2 * B), f32),
+            pltpu.VMEM((8, PIECE, T), f32),
+            pltpu.VMEM((4, PIECE, T), f32),
+            pltpu.VMEM((4, PIECE, T), f32),
+            pltpu.VMEM((3, PIECE, T), f32),
+            pltpu.VMEM((8, PIECE, T), f32),
+            pltpu.VMEM((2, 16, 16, NB), f32),
+            pltpu.SemaphoreType.DMA((24,)),
+            pltpu.SemaphoreType.DMA((16,)),
         ],
-        compiler_params=pltpu.CompilerParams(vmem_limit_bytes=50 * 1024 * 1024),
+        compiler_params=pltpu.CompilerParams(
+            vmem_limit_bytes=50 * 1024 * 1024, collective_id=0, has_side_effects=True),
         name="factor",
-    )(g, a1)
+    )(panel)
 
 
 def mult(left, right):
@@ -177,11 +303,8 @@
     col_index = lax.axis_index("col")
     owner_row = col_index // fanout
     place = col_index % fanout * col_rows
-    gram = inner_rows(panel, panel)
-    top = jnp.where(row_index == 0, panel[:NB], jnp.zeros((NB, NB), jnp.float32))
-    gram, top = lax.psum((gram, top), "row")
     panel_cols = from_root(lax.dynamic_slice_in_dim(panel, place, col_rows, 0), "row", owner_row)
-    r_up, rit, lui, mi = factor(gram, top)
+    r_up, rit, lui, mi = factor(panel)
     k2 = mult(rit.T, lui.T)
     shifted = panel.at[:NB].add(jnp.where(row_index == 0, r_up, jnp.zeros_like(r_up)))
     shifted_cols = panel_cols + jnp.where(col_index == 0, r_up, jnp.zeros_like(r_up))

time: 390 us -> 399 us (1.023)
  Pallas kernels: 42.6 us -> 65.7 us
  waiting for transfers between devices: 269 us -> 252 us
    psum x1 -> x0, waiting for transfers between devices: 71.7 us -> none  [on_device(): gram, top = lax.psum((gram, top), 'row')]
    psum x1 -> x2, waiting for transfers between devices: 57.4 us -> 114 us  [from_root(): return lax.psum(block, axis)]
    pallas_call x1, Pallas kernels: 42.6 us -> 65.7 us  [factor(): pl.pallas_call(factor_kernel, out_shape=[sq] * 4, in_specs=[vm], out_spec...]
    dot_general x2 -> x1, matrix products: 11.2 us -> 6.71 us  [inner_rows(): lax.dot_general(left, right, (((0,), (0,)), ((), ())), precision=lax.Prec...]
  transfers between devices with their start and end apart: 4 -> 4, of which waited for: 4 -> 4; matrix products, arithmetic and copies ran while one was open for 4% -> 5% of each run, Pallas kernels for 0% -> 0%
where the time goes in v2:
time: 399 us; the launch traced here: 395 us
  waiting for transfers between devices  252 us (63%)
  Pallas kernels  65.7 us (16%)
  matrix products  52.1 us (13%)
  between operations  14.3 us (4%)
  local copies, waits for them, and re-layouts  5.93 us (1%)
  other arithmetic  4.34 us (1%)
    psum x2, waiting for transfers between devices, from_root(): return lax.psum(block, axis)  114 us
    psum x1, waiting for transfers between devices, on_device(): image_rows = lax.psum(mult(trailing, scaled_cols), 'col')  82.2 us
    pallas_call x1, Pallas kernels, factor(): pl.pallas_call(factor_kernel, out_shape=[sq] * 4, in_specs=[vm], out_spec...  65.7 us
    psum x1, waiting for transfers between devices, on_device(): curv = lax.psum(inner_rows(scaled_rows, image_rows), 'row')  55.7 us
    dot_general x7, matrix products, mult(): return jnp.dot(left, right, precision=lax.Precision.HIGHEST)  35.2 us
    dot_general x2, matrix products, outer_cols(): lax.dot_general(left, right, (((1,), (1,)), ((), ())), precision=lax.Prec...  10.1 us
  transfers between devices with their start and end apart: 4, of which 4 were waited for; matrix products, arithmetic and copies ran while one was open for 5% of the time, Pallas kernels for 0%

profile of v2, /device:TPU:0, one launch (start us, length us, event | category | flops | bytes accessed | tf_op | source)
XLA Modules:
  0.0 395.1 jit_solution(13224351604187748721)
XLA Ops:
  7.2 0.0 all-reduce.5.cloned.1.call-start
  7.2 3.1 copy.12.panel_ref
  10.3 65.7 %factor.1 = (f32[512,512]{1,0:T(8,128)S(1)}, f32[512,512]{1,0:T(8,128)S(1)}, f32[512,512]{1,0:T(8,128)S(1)}, f32[512,512]{1,0:T(8,128)}) custom-call(f32[1024,512]{1,0:T(8,128)} %copy.12.panel_ref), custom_call_target="tpu_custom_call" | custom-call | tf_op jit(solution)/shard_map/factor/pallas_call | solution.py:257
  76.0 3.2 dynamic-slice_select_fusion.1
  79.2 0.0 all-reduce.5.cloned.1.call-update
  79.2 0.0 all-reduce.7.cloned.1.call-start
  79.3 4.4 %fusion.5 = f32[512,512]{1,0:T(8,128)} fusion(f32[512,512]{1,0:T(8,128)S(1)} %get-tuple-element.20, f32[512,512]{1,0:T(8,128)S(1)} %get-tuple-element.21), kind=kOutput, calls=%fused_computation.12 | convolution fusion | flops 1610612736 | bytes 3145728 | tf_op jit(solution)/shard_map/dot_general | solution.py:282
  83.7 0.0 copy-start.4
  83.7 57.0 %all-reduce.5.cloned.1.call-done = f32[512,512]{1,0:T(8,128)} async-done(((f32[512,512]{1,0:T(8,128)}), f32[512,512]{1,0:T(8,128)}) %all-reduce.5.cloned.1.call-update) | async-done | bytes 1048592 | tf_op jit(solution)/shard_map/psum | solution.py:295
  140.7 3.4 fusion.1
  144.2 0.0 copy-done.4
  144.2 4.8 %convolution_bitcast_fusion = f32[1024,512]{1,0:T(8,128)} fusion(f32[512,512]{1,0:T(8,128)S(1)} %fusion.1, f32[1024,512]{1,0:T(8,128)S(1)} %copy-done.4), kind=kOutput, calls=%fused_computation.2 | convolution fusion | flops 3221225472 | bytes 5242880 | tf_op jit(solution)/shard_map/dot_general | solution.py:282
  149.0 0.0 copy-start
  149.0 0.0 all-reduce.7.cloned.1.call-update
  149.0 0.0 all-reduce.9.cloned.1.call-start
  149.0 1.5 copy-done
  150.6 6.0 %fusion.6 = f32[1024,512]{1,0:T(8,128)} fusion(f32[1024,512]{1,0:T(8,128)S(1)} %copy-done, f32[512,512]{1,0:T(8,128)} %fusion.5), kind=kOutput, calls=%fused_computation.13 | convolution fusion | flops 3221225472 | bytes 5242880 | tf_op jit(solution)/shard_map/dot_general | solution.py:282
  156.5 82.2 %all-reduce.7.cloned.1.call-done = f32[1024,512]{1,0:T(8,128)} async-done(((f32[1024,512]{1,0:T(8,128)}), f32[1024,512]{1,0:T(8,128)}) %all-reduce.7.cloned.1.call-update) | async-done | bytes 2097168 | tf_op jit(solution)/shard_map/psum | solution.py:315
  238.8 6.7 %fusion.7 = f32[512,512]{1,0:T(8,128)} fusion(f32[1024,512]{1,0:T(8,128)} %fusion.6, f32[1024,512]{1,0:T(8,128)} %all-reduce.7.cloned.1.call-done), kind=kOutput, calls=%fused_computation.14 | convolution fusion | flops 3221225472 | bytes 5242880 | tf_op jit(solution)/shard_map/dot_general | solution.py:286
  245.5 0.0 all-reduce.9.cloned.1.call-update
  245.5 0.3 all-reduce.11.cloned.1.call-start
  245.7 6.0 %fusion.4 = f32[1024,512]{1,0:T(8,128)} fusion(f32[1024,512]{1,0:T(8,128)S(1)} %copy-done, f32[512,512]{1,0:T(8,128)} %get-tuple-element.19), kind=kOutput, calls=%fused_computation.11 | convolution fusion | flops 3221225472 | bytes 5242880 | tf_op jit(solution)/shard_map/dot_general | solution.py:282
  251.7 55.7 %all-reduce.9.cloned.1.call-done = f32[512,512]{1,0:T(8,128)} async-done(((f32[512,512]{1,0:T(8,128)}), f32[512,512]{1,0:T(8,128)}) %all-reduce.9.cloned.1.call-update) | async-done | bytes 1048592 | tf_op jit(solution)/shard_map/psum | solution.py:316
  307.5 6.1 %multiply_subtract_fusion = f32[1024,512]{1,0:T(8,128)S(1)} fusion(f32[1024,512]{1,0:T(8,128)} %all-reduce.7.cloned.1.call-done, f32[1024,512]{1,0:T(8,128)} %fusion.4, f32[512,512]{1,0:T(8,128)} %all-reduce.9.cloned.1.call-done), kind=kOutput, calls=%fused_computation.1 | convolution fusion | flops 3222274048 | bytes 7340032 | tf_op jit(solution)/shard_map/dot_general | solution.py:282
  313.5 0.0 copy-start.2
  313.6 1.3 copy-done.2
  314.9 1.1 dynamic-slice_select_fusion
  316.0 0.0 all-reduce.11.cloned.1.call-update
  316.0 0.0 copy-start.1
  316.0 4.5 %fusion = f32[512,512]{1,0:T(8,128)} fusion(f32[512,512]{1,0:T(8,128)} %get-tuple-element.19, f32[512,512]{1,0:T(8,128)} %all-reduce.5.cloned.1.call-done, f32[512,512]{1,0:T(8,128)S(1)} %get-tuple-element.18, pred[]{:T(512)S(6)} %eq.14), kind=kOutput, calls=%fused_computation.7 | convolution fusion | flops 1611137024 | bytes 4194305 | tf_op jit(solution)/shard_map/dot_general | solution.py:282
  320.5 0.0 copy-start.6
  320.5 57.4 %all-reduce.11.cloned.1.call-done = f32[512,512]{1,0:T(8,128)} async-done(((f32[512,512]{1,0:T(8,128)}), f32[512,512]{1,0:T(8,128)}) %all-reduce.11.cloned.1.call-update) | async-done | bytes 1048592 | tf_op jit(solution)/shard_map/psum | solution.py:295
  377.9 0.0 copy-done.1
  377.9 0.0 copy-start.3
  378.0 0.0 copy-start.5
  378.0 4.8 %fusion.8 = f32[1024,512]{1,0:T(8,128)S(1)} fusion(f32[1024,512]{1,0:T(8,128)S(1)} %copy-done.1, f32[512,512]{1,0:T(8,128)} %all-reduce.11.cloned.1.call-done), kind=kOutput, calls=%fused_computation.15 | convolution fusion | flops 3221225472 | bytes 5242880 | tf_op jit(solution)/shard_map/dot_general | solution.py:290
  382.8 0.0 copy-done.6
  382.8 0.0 copy-done.3
  382.8 0.0 copy-done.5
  382.8 5.3 %subtract_subtract_fusion = f32[1024,512]{1,0:T(8,128)} fusion(f32[1024,512]{1,0:T(8,128)S(1)} %copy-done.5, f32[1024,512]{1,0:T(8,128)S(1)} %fusion.8, f32[1024,512]{1,0:T(8,128)S(1)} %copy-done.3, f32[512,512]{1,0:T(8,128)S(1)} %copy-done.6), kind=kOutput, calls=%fused_computation | convolution fusion | flops 3222274048 | bytes 9437184 | tf_op jit(solution)/shard_map/dot_general | solution.py:290
Async XLA Ops:
  7.2 133.6 %all-reduce.5.cloned.1.call-start = ((), (), s32[]{:S(2)}) async-start(), calls=%async_computation | async-start | bytes 2097152 | tf_op jit(solution)/shard_map/psum | solution.py:295
  79.2 159.5 %all-reduce.7.cloned.1.call-start = ((), (), s32[]{:S(2)}) async-start(), calls=%async_computation.1 | async-start | bytes 4194304 | tf_op jit(solution)/shard_map/psum | solution.py:315
  83.7 60.4 %copy-start.4 = (f32[1024,512]{1,0:T(8,128)S(1)}, f32[1024,512]{1,0:T(8,128)}, u32[]{:S(2)}) copy-start(f32[1024,512]{1,0:T(8,128)} %param.5) | copy-start | bytes 6291460
  149.0 1.6 copy-start
  149.0 158.5 %all-reduce.9.cloned.1.call-start = ((), (), s32[]{:S(2)}) async-start(), calls=%async_computation.2 | async-start | bytes 2097152 | tf_op jit(solution)/shard_map/psum | solution.py:316
  245.5 132.5 %all-reduce.11.cloned.1.call-start = ((), (), s32[]{:S(2)}) async-start(), calls=%async_computation.3 | async-start | bytes 2097152 | tf_op jit(solution)/shard_map/psum | solution.py:295
  313.5 1.3 copy-start.2
  316.0 61.9 %copy-start.1 = (f32[1024,512]{1,0:T(8,128)S(1)}, f32[1024,512]{1,0:T(8,128)}, u32[]{:S(2)}) copy-start(f32[1024,512]{1,0:T(8,128)} %fusion.4) | copy-start | bytes 6291460
  320.5 62.3 %copy-start.6 = (f32[512,512]{1,0:T(8,128)S(1)}, f32[512,512]{1,0:T(8,128)}, u32[]{:S(2)}) copy-start(f32[512,512]{1,0:T(8,128)} %fusion) | copy-start | bytes 3145732
  377.9 4.9 %copy-start.3 = (f32[1024,512]{1,0:T(8,128)S(1)}, f32[1024,512]{1,0:T(8,128)}, u32[]{:S(2)}) copy-start(f32[1024,512]{1,0:T(8,128)} %copy-done.2) | copy-start | bytes 6291460
  378.0 4.9 %copy-start.5 = (f32[1024,512]{1,0:T(8,128)S(1)}, f32[1024,512]{1,0:T(8,128)}, u32[]{:S(2)}) copy-start(f32[1024,512]{1,0:T(8,128)} %param.5) | copy-start | bytes 6291460
Sparse Core Ops, SparseCore 0:
  79.3 61.3 all-reduce.4
  149.1 89.5 all-reduce.6
  245.6 61.8 all-reduce.8
  316.1 61.7 all-reduce.10
